TPU v7x, 32 devices: a whole 2x2x4 slice. The times are simulated.
32 devices in a mesh: layout: 2 (over x), tile: 16 (over z, y, core).
Axes of the slice: x: 2, y: 2, z: 4, core: 2. Of those that a mesh axis runs over, the one named last changes fastest.
Arguments:
- velocity: float32 [2, 3, 4, 512, 256], P('layout', None, None, 'tile'), may hold values from -1.2 to 2.2, as said below
- inflow: float32 [2, 3, 4, 256], P('layout'), may hold values from -1.2 to 2.2, as said below
- turbine_site: int32 [2, 40], P('layout'), may hold values from 0 to 47, as said below
- turbine_block: int32 [2, 40], P('layout'), may hold values from 0 to 63, as said below
- turbine_slot: int32 [2, 40], P('layout'), may hold values from 0 to 47, as said below
- smear: float32 [2, 48, 512], P('layout', 'tile'), may hold values from 0.2 to 2
- yaw: float32 [2, 48], P('layout', 'tile'), may hold values from -0.5 to 0.5
- thrust_coef: float32 [2, 48], P('layout', 'tile'), may hold values from 0.5 to 1.5
Outputs:
- velocity_out: float32 [2, 3, 4, 512, 256], P('layout', None, None, 'tile')
- slot_power: float32 [2, 48], P('layout', 'tile')
Inputs may be any that keep to these rules, and one draw needn't show every extreme that they name: `turbine_site`: within a layout all sites differ; the tile of site s is s // 3; in every layout some tile holds exactly 3 turbines. `turbine_block`: blocks are numbered x-block times (8) plus y-block; turbines of one tile have different blocks. `turbine_slot`: within a layout all slots differ; the owner tile of slot s is s // 3; in every layout some tile owns exactly 3 turbines; slots that no turbine names are empty. `velocity`: component 0 lies within 1 - 1.2 and 1 + 1.2, components 1 and 2 within -1.2 and 1.2. `inflow`: component 0 lies within 1 - 1.2 and 1 + 1.2, components 1 and 2 within -1.2 and 1.2.
All inputs are finite; a program needn't handle non-finite values.
Results may differ from a plain program's by a relative error of at most 0.0003.
Values sent between devices are 32-bit elements; how exact they have to be, the bound alone decides.
A program may use at most 64 MiB of HBM per device.

v0:
```python
import jax
import jax.numpy as jnp
from jax import lax
from jax.sharding import PartitionSpec as P

BX = 4
BY = 32
HOME_MOST = 3
OWN_SLOTS = 3
STEP_LAY = 1


time_step = 0.1
smag_coef = 0.0256
strain_floor = 0.01


def from_root(shard, axis, root):
    mine = lax.axis_index(axis) == root
    return lax.psum(jnp.where(mine, shard, jnp.zeros_like(shard)), axis)


def extended(shard, sides, width):
    for axis, dim in sides:
        count, length = (lax.axis_size(axis), shard.shape[dim])
        up = [(i, (i + 1) % count) for i in range(count - 1)]
        down = [(j, i) for i, j in up]
        last = lax.slice_in_dim(shard, length - width, length, axis=dim)
        initial = lax.slice_in_dim(shard, 0, width, axis=dim)
        before = lax.ppermute(last, axis, up)
        after = lax.ppermute(initial, axis, down)
        shard = jnp.concatenate([before, shard, after], axis=dim)
    return shard


def advance(x_padded):
    wrapped = jnp.concatenate([x_padded[..., -1:], x_padded, x_padded[..., :1]], axis=3)
    padded = jnp.concatenate([wrapped[:, :1], wrapped, wrapped[:, -1:]], axis=1)
    centre = padded[:, 1:-1, 1:-1, 1:-1]
    x_minus = padded[:, 1:-1, :-2, 1:-1]
    x_plus = padded[:, 1:-1, 2:, 1:-1]
    y_minus = padded[:, 1:-1, 1:-1, :-2]
    y_plus = padded[:, 1:-1, 1:-1, 2:]
    z_minus = padded[:, :-2, 1:-1, 1:-1]
    z_plus = padded[:, 2:, 1:-1, 1:-1]
    grad_x = 0.5 * (x_plus - x_minus)
    grad_y = 0.5 * (y_plus - y_minus)
    grad_z = 0.5 * (z_plus - z_minus)
    shear_xy = grad_y[0] + grad_x[1]
    shear_xz = grad_z[0] + grad_x[2]
    shear_yz = grad_z[1] + grad_y[2]
    strain_sq = 2.0 * (grad_x[0] * grad_x[0] + grad_y[1] * grad_y[1] + grad_z[2] * grad_z[2])
    strain_sq = strain_sq + shear_xy * shear_xy + shear_xz * shear_xz + shear_yz * shear_yz
    viscosity = smag_coef * jnp.sqrt(strain_sq + strain_floor)
    laplace = x_plus + x_minus + y_plus + y_minus + z_plus + z_minus - 6.0 * centre
    along_x = centre[0]
    along_y = centre[1]
    along_z = centre[2]
    upwind = jnp.maximum(along_x, 0.0) * (centre - x_minus) + jnp.minimum(along_x, 0.0) * (
        x_plus - centre
    )
    upwind = (
        upwind
        + jnp.maximum(along_y, 0.0) * (centre - y_minus)
        + jnp.minimum(along_y, 0.0) * (y_plus - centre)
    )
    upwind = (
        upwind
        + jnp.maximum(along_z, 0.0) * (centre - z_minus)
        + jnp.minimum(along_z, 0.0) * (z_plus - centre)
    )
    return centre + time_step * (viscosity * laplace - upwind)


def rotor_forces(blocks, weights, angles, thrust_coefs, present):
    cosine = jnp.cos(angles)[:, None]
    sine_part = jnp.sin(angles)[:, None]
    normal = blocks[:, 0] * cosine + blocks[:, 1] * sine_part
    weight_sum = jnp.where(present, jnp.sum(weights, axis=1), 1.0)
    disk_speed = jnp.sum(weights * normal, axis=1) / weight_sum
    thrust = -0.5 * thrust_coefs * disk_speed * jnp.abs(disk_speed)
    spread = thrust[:, None] * weights
    forces = jnp.stack([spread * cosine, spread * sine_part], axis=1)
    powers = 0.5 * thrust_coefs * jnp.abs(disk_speed) * disk_speed * disk_speed
    return (forces, powers)


def matching(key_list, row_count):
    row_ids = jnp.arange(row_count, dtype=jnp.int32)
    return (key_list[:, None] == row_ids[None, :]).astype(jnp.float32)


def select_rows(pick, key_list, shard_rows):
    chooser = jnp.dot(
        pick, matching(key_list, shard_rows.shape[0]), precision=lax.Precision.HIGHEST
    )
    return jnp.einsum("or,r...->o...", chooser, shard_rows, precision=lax.Precision.HIGHEST)


def local(velocity, inflow, turbine_site, turbine_block, turbine_slot, smear, yaw, thrust_coef):
    current = velocity[0]
    levels = current.shape[1]
    width_x = current.shape[2]
    width_y = current.shape[3]
    tile_index = lax.axis_index("tile")
    tile_count = lax.axis_size("tile")
    step_count = STEP_LAY * lax.axis_size("layout")
    site_list = turbine_site[0]
    blocks_of = turbine_block[0]
    slot_list = turbine_slot[0]
    home_rows = tile_index * HOME_MOST + jnp.arange(HOME_MOST, dtype=jnp.int32)
    own_rows = tile_index * OWN_SLOTS + jnp.arange(OWN_SLOTS, dtype=jnp.int32)
    home_pick = (site_list[None, :] == home_rows[:, None]).astype(jnp.float32)
    own_pick = (slot_list[None, :] == own_rows[:, None]).astype(jnp.float32)
    home_block = jnp.sum(jnp.where(home_pick > 0, blocks_of[None, :], 0), axis=1)
    y_blocks = width_y // BY
    x_start = home_block // y_blocks * BX
    y_start = home_block % y_blocks * BY
    cell_count = levels * BX * BY
    zero_index = jnp.zeros((), jnp.int32)
    power_total = jnp.zeros((OWN_SLOTS,), jnp.float32)
    for step_index in range(step_count):
        inflow_now = from_root(inflow[step_index % STEP_LAY], "layout", step_index // STEP_LAY)
        x_padded = extended(current, (("tile", 2),), 1)
        left_cells = jnp.where(tile_index == 0, inflow_now[:, :, None, :], x_padded[:, :, :1])
        right_cells = jnp.where(
            tile_index == tile_count - 1, current[:, :, -1:], x_padded[:, :, -1:]
        )
        x_padded = jnp.concatenate([left_cells, current, right_cells], axis=2)
        stepped = advance(x_padded)
        source = current[:2]

        def take_one(x_first, y_first):
            return lax.dynamic_slice(
                source, (zero_index, zero_index, x_first, y_first), (2, levels, BX, BY)
            ).reshape(2, cell_count)

        disk_blocks = jax.vmap(take_one)(x_start, y_start)
        owned_blocks = select_rows(
            own_pick, site_list, lax.all_gather(disk_blocks, "tile", axis=0, tiled=True)
        )
        owned_force, power_now = rotor_forces(
            owned_blocks, smear[0], yaw[0], thrust_coef[0], jnp.ones((OWN_SLOTS,), jnp.bool_)
        )
        home_force = select_rows(
            home_pick, slot_list, lax.all_gather(owned_force, "tile", axis=0, tiled=True)
        )
        power_total = power_total + power_now
        spread = jnp.zeros((2, levels, width_x, width_y), jnp.float32)
        for slot_index in range(HOME_MOST):
            where_at = (zero_index, zero_index, x_start[slot_index], y_start[slot_index])
            existing = lax.dynamic_slice(spread, where_at, (2, levels, BX, BY))
            spread = lax.dynamic_update_slice(
                spread, existing + home_force[slot_index].reshape(2, levels, BX, BY), where_at
            )
        current = jnp.concatenate([stepped[:2] + time_step * spread, stepped[2:]], axis=0)
    power_out = power_total / step_count
    return (current[None], power_out[None])


def solution(mesh):
    in_specs = (
        P("layout", None, None, "tile", None),
        P("layout", None, None, None),
        P("layout", None),
        P("layout", None),
        P("layout", None),
        P("layout", "tile", None),
        P("layout", "tile"),
        P("layout", "tile"),
    )
    out_specs = (P("layout", None, None, "tile", None), P("layout", "tile"))
    return jax.shard_map(local, mesh=mesh, in_specs=in_specs, out_specs=out_specs, check_vma=False)
```

profile of v0, /device:TPU:0, one launch (start us, length us, event | category | flops | bytes accessed | tf_op | source)
XLA Modules:
  0.0 160.6 jit_solution(14355523402170757389)
XLA Ops:
  0.7 0.9 slice.318
  1.6 1.3 collective-permute-start
  2.9 1.0 slice.261
  3.9 0.9 convolution_bitcast_fusion
  4.8 0.9 convolution_bitcast_fusion.1
  5.6 0.9 select_reduce_fusion
  6.5 0.6 fusion.102
  14.5 1.1 maximum_bitcast_fusion.6
  15.6 5.9 %copy.317 = f32[1,2,4,32,256]{2,1,4,3,0:T(2,128)} copy(f32[1,2,4,32,256]{4,3,2,1,0:T(8,128)S(1)} %slice.261) | data formatting | bytes 524288
  21.5 4.4 %gather_fusion = f32[3,2,4,4,32]{2,1,4,3,0:T(2,128)S(1)} fusion(f32[2,4,32,256]{1,0,3,2:T(2,128)} %bitcast.150, s32[3]{0:T(128)S(1)} %fusion.94), kind=kCustom, calls=%fused_computation | custom fusion | bytes 24624 | tf_op jit(solution)/shard_map/vmap()/gather | solution.py:134
  25.9 0.2 copy.297
  26.3 24.3 %all_gather.12 = f32[48,2,512]{2,1,0:T(2,128)S(1)} all-gather(f32[3,2,512]{2,1,0:T(2,128)S(1)} %reshape.430), channel_id=1, replica_groups=mesh['layout'=2,'tile'=16] {'tile'}, dimensions={0}, use_global_device_ids=true | all-gather | bytes 208896 | tf_op jit(solution)/shard_map/all_gather | solution.py:140
  50.6 0.2 fusion.27
  50.9 0.2 fusion.69
  51.2 18.0 %all_gather.13 = f32[48,2,512]{2,1,0:T(2,128)S(1)} all-gather(f32[3,2,512]{2,1,0:T(2,128)S(1)} %pad_maximum_fusion.17), channel_id=1, replica_groups=mesh['layout'=2,'tile'=16] {'tile'}, dimensions={0}, use_global_device_ids=true | all-gather | bytes 208896 | tf_op jit(solution)/shard_map/all_gather | solution.py:146
  69.2 0.2 fusion.25
  72.2 2.7 %dynamic_update_slice.18 = f32[2,4,32,256]{3,2,1,0:T(8,128)S(1)} dynamic-update-slice(f32[2,4,32,256]{3,2,1,0:T(8,128)S(1)} %broadcast.389.clone, f32[2,4,4,32]{3,2,1,0:T(4,128)S(1)} %reshape_squeeze.18, s32[]{:T(128)} %constant.24.clone.1, s32[]{:T(128)} %constant.24.clone.1, s32[]{:T(128)S(6)} %select_n.146, s32[]{:T(128)S(6)} %select_n.148) | dynamic-update-slice | bytes 8196 | tf_op jit(solution)/shard_map/dynamic_update_slice | solution.py:153
  74.9 2.7 %dynamic_update_slice.19 = f32[2,4,32,256]{3,2,1,0:T(8,128)S(1)} dynamic-update-slice(f32[2,4,32,256]{3,2,1,0:T(8,128)S(1)} %dynamic_update_slice.18, f32[2,4,4,32]{3,2,1,0:T(4,128)S(1)} %dynamic-slice_add_fusion.3, s32[]{:T(128)} %constant.24.clone.1, s32[]{:T(128)} %constant.24.clone.1, s32[]{:T(128)S(6)} %select_n.149, s32[]{:T(128)S(6)} %select_n.150) | dynamic-update-slice | bytes 8196 | tf_op jit(solution)/shard_map/dynamic_update_slice | solution.py:153
  79.0 2.7 %dynamic_update_slice.20 = f32[2,4,32,256]{3,2,1,0:T(8,128)S(1)} dynamic-update-slice(f32[2,4,32,256]{3,2,1,0:T(8,128)S(1)} %dynamic_update_slice.19, f32[2,4,4,32]{3,2,1,0:T(4,128)S(1)} %dynamic-slice_add_fusion.2, s32[]{:T(128)} %constant.24.clone.1, s32[]{:T(128)} %constant.24.clone.1, s32[]{:T(128)S(6)} %select_n.151, s32[]{:T(128)S(6)} %select_n.152) | dynamic-update-slice | bytes 8196 | tf_op jit(solution)/shard_map/dynamic_update_slice | solution.py:153
  81.8 1.3 collective-permute-start.1
  83.1 9.3 %all-reduce = (f32[3,4,1,256]{3,2,1,0:T(1,128)S(1)}, f32[3,4,1,256]{3,2,1,0:T(1,128)S(1)}) all-reduce(f32[3,4,1,256]{3,2,1,0:T(1,128)S(1)} %get-tuple-element.50, f32[3,4,1,256]{3,2,1,0:T(1,128)S(1)} %get-tuple-element.49), channel_id=1, replica_groups=mesh['layout'=2,'tile'=16] {'layout'}, use_global_device_ids=true, to_apply=%region_4.5 | all-reduce | flops 6144 | bytes 49152 | tf_op jit(solution)/shard_map/psum | solution.py:20
  92.4 0.3 copy_dynamic-update-slice_fusion.1
  92.9 0.5 pad_maximum_fusion
  93.4 0.2 fusion.99
  93.7 0.6 pad_maximum_fusion.14
  94.5 0.3 fusion.12
  95.0 0.6 fusion.11
  95.7 5.9 %copy.310 = f32[2,4,32,256]{1,0,3,2:T(2,128)} copy(f32[2,4,32,256]{3,2,1,0:T(8,128)S(1)} %slice_add_fusion.1) | data formatting | bytes 524288 | tf_op jit(solution)/shard_map/add | solution.py:156
  101.6 4.4 %gather_fusion.1 = f32[3,2,4,4,32]{2,1,4,3,0:T(2,128)S(1)} fusion(f32[2,4,32,256]{1,0,3,2:T(2,128)} %copy.310, s32[3]{0:T(128)S(1)} %fusion.94), kind=kCustom, calls=%fused_computation.1 | custom fusion | bytes 24624 | tf_op jit(solution)/shard_map/vmap()/gather | solution.py:134
  106.1 0.2 copy.311
  106.4 19.2 %all_gather.14 = f32[48,2,512]{2,1,0:T(2,128)S(1)} all-gather(f32[3,2,512]{2,1,0:T(2,128)S(1)} %reshape.431), channel_id=1, replica_groups=mesh['layout'=2,'tile'=16] {'tile'}, dimensions={0}, use_global_device_ids=true | all-gather | bytes 208896 | tf_op jit(solution)/shard_map/all_gather | solution.py:140
  125.6 0.2 fusion.23
  125.8 0.2 fusion.64
  126.0 0.5 fusion.95
  126.6 18.2 %all_gather.15 = f32[48,2,512]{2,1,0:T(2,128)S(1)} all-gather(f32[3,2,512]{2,1,0:T(2,128)S(1)} %pad_maximum_fusion.18), channel_id=1, replica_groups=mesh['layout'=2,'tile'=16] {'tile'}, dimensions={0}, use_global_device_ids=true | all-gather | bytes 208896 | tf_op jit(solution)/shard_map/all_gather | solution.py:146
  144.9 0.2 fusion.21
  145.3 1.3 collective-permute-start.2
  146.7 2.7 %dynamic_update_slice.21 = f32[2,4,32,256]{3,2,1,0:T(8,128)S(1)} dynamic-update-slice(f32[2,4,32,256]{3,2,1,0:T(8,128)S(1)} %broadcast.389, f32[2,4,4,32]{3,2,1,0:T(4,128)S(1)} %reshape_squeeze.21, s32[]{:T(128)} %constant.24.clone.1, s32[]{:T(128)} %constant.24.clone.1, s32[]{:T(128)S(6)} %select_n.146, s32[]{:T(128)S(6)} %select_n.148) | dynamic-update-slice | bytes 8196 | tf_op jit(solution)/shard_map/dynamic_update_slice | solution.py:153
  149.4 2.7 %dynamic_update_slice.22 = f32[2,4,32,256]{3,2,1,0:T(8,128)S(1)} dynamic-update-slice(f32[2,4,32,256]{3,2,1,0:T(8,128)S(1)} %dynamic_update_slice.21, f32[2,4,4,32]{3,2,1,0:T(4,128)S(1)} %dynamic-slice_add_fusion.1, s32[]{:T(128)} %constant.24.clone.1, s32[]{:T(128)} %constant.24.clone.1, s32[]{:T(128)S(6)} %select_n.149, s32[]{:T(128)S(6)} %select_n.150) | dynamic-update-slice | bytes 8196 | tf_op jit(solution)/shard_map/dynamic_update_slice | solution.py:153
  152.2 1.5 collective-permute-start.3
  153.8 2.7 %dynamic_update_slice.23 = f32[2,4,32,256]{3,2,1,0:T(8,128)S(1)} dynamic-update-slice(f32[2,4,32,256]{3,2,1,0:T(8,128)S(1)} %dynamic_update_slice.22, f32[2,4,4,32]{3,2,1,0:T(4,128)S(1)} %dynamic-slice_add_fusion, s32[]{:T(128)} %constant.24.clone.1, s32[]{:T(128)} %constant.24.clone.1, s32[]{:T(128)S(6)} %select_n.151, s32[]{:T(128)S(6)} %select_n.152) | dynamic-update-slice | bytes 8196 | tf_op jit(solution)/shard_map/dynamic_update_slice | solution.py:153
  156.6 0.3 copy_dynamic-update-slice_fusion
  157.1 0.5 pad_maximum_fusion.1
  157.7 0.2 fusion.98
  157.9 0.6 pad_maximum_fusion.6
  158.7 0.3 subtract_multiply_fusion
  159.1 0.6 multiply_add_fusion
  159.8 0.8 maximum_bitcast_fusion
  (69 shorter events, 3.2 us)
Async XLA Ops:
  0.6 81.1 %copy-start = (f32[1,3,4,32,256]{4,3,2,1,0:T(8,128)S(1)}, f32[1,3,4,32,256]{4,3,2,1,0:T(8,128)}, u32[]{:S(2)}) copy-start(f32[1,3,4,32,256]{4,3,2,1,0:T(8,128)} %param.8) | copy-start | bytes 1179652
  0.6 49.9 %copy-start.4 = (f32[1,3]{1,0:T(1,128)S(1)}, f32[1,3]{1,0:T(1,128)}, u32[]{:S(2)}) copy-start(f32[1,3]{1,0:T(1,128)} %param.14) | copy-start | bytes 40
  0.7 50.1 %copy-start.1 = (f32[1,3,512]{2,0,1:T(1,128)S(1)}, f32[1,3,512]{2,0,1:T(1,128)}, u32[]{:S(2)}) copy-start(f32[1,3,512]{2,0,1:T(1,128)} %param.13) | copy-start | bytes 18436
  0.7 50.4 %copy-start.3 = (f32[1,3]{1,0:T(1,128)S(1)}, f32[1,3]{1,0:T(1,128)}, u32[]{:S(2)}) copy-start(f32[1,3]{1,0:T(1,128)} %param.15) | copy-start | bytes 40
  0.7 78.2 %copy-start.2 = (f32[1,3,4,256]{3,2,1,0:T(4,128)S(1)}, f32[1,3,4,256]{3,2,1,0:T(4,128)}, u32[]{:S(2)}) copy-start(f32[1,3,4,256]{3,2,1,0:T(4,128)} %param.9) | copy-start | bytes 36868
  1.6 80.1 %collective-permute-start = (f32[3,4,1,256]{3,2,1,0:T(1,128)S(1)}, f32[3,4,1,256]{3,2,1,0:T(1,128)S(1)}, u32[]{:S(2)}, u32[]{:S(2)}) collective-permute-start(f32[3,4,1,256]{3,2,1,0:T(1,128)S(1)} %slice.318), channel_id=1, source_target_pairs={{1,0},{2,1},{3,2},{4,3},{5,4},{6,5},{7,6},{8,7},{9,8},{10,9},{11,1... | collective-permute-start | bytes 36872 | tf_op jit(solution)/shard_map/ppermute | solution.py:31
  81.8 10.6 %collective-permute-start.1 = (f32[3,4,1,256]{3,2,1,0:T(1,128)S(1)}, f32[3,4,1,256]{3,2,1,0:T(1,128)S(1)}, u32[]{:S(2)}, u32[]{:S(2)}) collective-permute-start(f32[3,4,1,256]{3,2,1,0:T(1,128)S(1)} %get-tuple-element.44), channel_id=1, source_target_pairs={{0,1},{1,2},{2,3},{3,4},{4,5},{5,6},{6,7},{7,8},{8,9},{9,10},{10,1... | collective-permute-start | bytes 36872 | tf_op jit(solution)/shard_map/ppermute | solution.py:30
  145.3 6.9 %collective-permute-start.2 = (f32[3,4,1,256]{3,2,1,0:T(1,128)S(1)}, f32[3,4,1,256]{3,2,1,0:T(1,128)S(1)}, u32[]{:S(2)}, u32[]{:S(2)}) collective-permute-start(f32[3,4,1,256]{3,2,1,0:T(1,128)S(1)} %fusion.56), channel_id=1, source_target_pairs={{1,0},{2,1},{3,2},{4,3},{5,4},{6,5},{7,6},{8,7},{9,8},{10,9},{11,1... | collective-permute-start | bytes 36872 | tf_op jit(solution)/shard_map/ppermute | solution.py:31
  152.2 4.2 %collective-permute-start.3 = (f32[3,4,1,256]{3,2,1,0:T(1,128)S(1)}, f32[3,4,1,256]{3,2,1,0:T(1,128)S(1)}, u32[]{:S(2)}, u32[]{:S(2)}) collective-permute-start(f32[3,4,1,256]{3,2,1,0:T(1,128)S(1)} %get-tuple-element.17), channel_id=1, source_target_pairs={{0,1},{1,2},{2,3},{3,4},{4,5},{5,6},{6,7},{7,8},{8,9},{9,10},{10,1... | collective-permute-start | bytes 36872 | tf_op jit(solution)/shard_map/ppermute | solution.py:30
where the time goes:
time: 162 us; the launch traced here: 161 us
  blocking collectives  89 us (55%)
  local copies, waits for them, and re-layouts  42.1 us (26%)
  between operations  12.2 us (8%)
  other arithmetic  9.35 us (6%)
  starting transfers between devices  5.33 us (3%)
  matrix products  2.63 us (2%)
    all_gather x2, blocking collectives, local(): lax.all_gather(disk_blocks, 'tile', axis=0, tiled=True)  43.4 us
    all_gather x2, blocking collectives, local(): lax.all_gather(owned_force, 'tile', axis=0, tiled=True)  36.2 us
    dynamic_update_slice x6, local copies, waits for them, and re-layouts, local(): lax.dynamic_update_slice(spread, existing + home_force[slot_index].reshap...  16 us
    psum x1, blocking collectives, from_root(): return lax.psum(jnp.where(mine, shard, jnp.zeros_like(shard)), axis)  9.34 us
    gather x4, local copies, waits for them, and re-layouts, take_one(): lax.dynamic_slice(source, (zero_index, zero_index, x_first, y_first), (2,...  9.3 us
    unnamed x15, local copies, waits for them, and re-layouts  6.47 us
    add x1, local copies, waits for them, and re-layouts, local(): stepped[:2] + time_step * spread  5.88 us
  transfers between devices with their start and end apart: 4, of which 0 were waited for; matrix products, arithmetic and copies ran while one was open for 21% of the time, Pallas kernels for 0%

commit v1 on v0

v1 whole, which is shorter than its diff:
```python
import functools

import jax
import jax.numpy as jnp
from jax import lax
from jax.experimental import pallas as pl
from jax.experimental.pallas import tpu as pltpu
from jax.sharding import PartitionSpec as P

BX = 4
BY = 32
HOME_MOST = 3
OWN_SLOTS = 3
LANES = 128
ROWS = 8

TIME_STEP = 0.1
SMAG = 0.0256
FLOOR = 0.01

MESH = pl.DeviceIdType.MESH


def kernel(
    tiles, layouts, levels, width_x, halves, turbines,
    vel_ref, inflow_ref, site_ref, block_ref, slot_ref, smear_ref, yaw_ref, coef_ref,
    out_ref, power_ref,
    q, site_s, block_s, slot_s, smear_v, yaw_v, coef_v, gathered, weights_v,
    planes, edge_out, edge_in, powers, power_v,
    local_sem, gather_send, gather_recv, plane_send, plane_recv,
    edge_send, edge_recv, power_send, power_recv,
):
    tile = lax.axis_index("tile")
    layout = lax.axis_index("layout")
    steps = layouts
    fields = 3 * levels
    x_tiles = width_x // ROWS
    first = ROWS
    y_blocks = halves * LANES // BY
    segs = LANES // BY

    def tile_at(distance):
        return lax.rem(tile + distance, tiles)

    def layout_at(distance):
        return lax.rem(layout + distance, layouts)

    barrier = pltpu.get_barrier_semaphore()
    for d in range(1, tiles):
        pl.semaphore_signal(
            barrier, inc=1, device_id=(layout, tile_at(d)), device_id_type=MESH
        )
    for d in range(1, layouts):
        pl.semaphore_signal(
            barrier, inc=1, device_id=(layout_at(d), tile), device_id_type=MESH
        )

    loads = [
        pltpu.make_async_copy(smear_ref.at[0], smear_v, local_sem.at[0]),
        pltpu.make_async_copy(yaw_ref, yaw_v, local_sem.at[1]),
        pltpu.make_async_copy(coef_ref, coef_v, local_sem.at[2]),
    ]
    field_loads = [
        pltpu.make_async_copy(
            vel_ref.at[0, :, :, :, pl.ds(h * LANES, LANES)],
            q.at[0, :, :, h, pl.ds(first, width_x), :],
            local_sem.at[3 + h],
        )
        for h in range(halves)
    ]
    base = 3 + halves
    plane_load = pltpu.make_async_copy(
        inflow_ref.at[0], planes.at[layout], local_sem.at[base]
    )
    list_loads = [
        pltpu.make_async_copy(site_ref, site_s, local_sem.at[base + 1]),
        pltpu.make_async_copy(block_ref, block_s, local_sem.at[base + 2]),
        pltpu.make_async_copy(slot_ref, slot_s, local_sem.at[base + 3]),
    ]
    for copy in loads + field_loads + [plane_load] + list_loads:
        copy.start()

    for copy in loads:
        copy.wait()
    lane1 = lax.broadcasted_iota(jnp.int32, (1, LANES), 1)
    for j in range(OWN_SLOTS):
        total = jnp.zeros((1, 1), jnp.float32)
        for l in range(levels):
            row = smear_v[pl.ds(j, 1), pl.ds(l * LANES, LANES)]
            gathered[tile, pl.ds(j * levels + l, 1), :] = row
            total = total + jnp.sum(row, axis=1, keepdims=True)
        angle = yaw_v[:, j : j + 1]
        packed = jnp.where(lane1 == 0, jnp.cos(angle), 0.0)
        packed = jnp.where(lane1 == 1, jnp.sin(angle), packed)
        packed = jnp.where(lane1 == 2, coef_v[:, j : j + 1], packed)
        packed = jnp.where(lane1 == 3, 1.0 / total, packed)
        gathered[tile, pl.ds(OWN_SLOTS * levels + j, 1), :] = packed

    for copy in field_loads:
        copy.wait()

    def pack_edge(step, side):
        row = first if side == 0 else first + width_x - 1
        for c in range(3):
            for l in range(levels):
                for h in range(halves):
                    i = (c * levels + l) * halves + h
                    edge_out[step, side, pl.ds(i, 1), :] = q[
                        step % 2, c, l, h, pl.ds(row, 1), :
                    ]

    def edge_copy(step, side):
        target = tile - 1 if side == 0 else tile + 1
        return pltpu.make_async_remote_copy(
            src_ref=edge_out.at[step, side],
            dst_ref=edge_in.at[step, 1 - side],
            send_sem=edge_send.at[step, side],
            recv_sem=edge_recv.at[step, 1 - side],
            device_id=(layout, target),
            device_id_type=MESH,
        )

    def send_edges(step):
        @pl.when(tile > 0)
        def _():
            edge_copy(step, 0).start()

        @pl.when(tile < tiles - 1)
        def _():
            edge_copy(step, 1).start()

    pack_edge(0, 0)
    pack_edge(0, 1)
    plane_load.wait()

    pl.semaphore_wait(barrier, tiles - 1 + layouts - 1)

    send_edges(0)

    def plane_copy(d):
        return pltpu.make_async_remote_copy(
            src_ref=planes.at[layout],
            dst_ref=planes.at[layout],
            send_sem=plane_send.at[d],
            recv_sem=plane_recv.at[d],
            device_id=(layout_at(d), tile),
            device_id_type=MESH,
        )

    @pl.when(tile == 0)
    def _():
        for d in range(1, layouts):
            plane_copy(d).start()

    def gather_copy(d):
        return pltpu.make_async_remote_copy(
            src_ref=gathered.at[tile],
            dst_ref=gathered.at[tile],
            send_sem=gather_send.at[d],
            recv_sem=gather_recv.at[d],
            device_id=(layout, tile_at(d)),
            device_id_type=MESH,
        )

    for d in range(1, tiles):
        gather_copy(d).start()

    for copy in list_loads:
        copy.wait()
    home_slot = [jnp.int32(0)] * HOME_MOST
    home_block = [jnp.int32(0)] * HOME_MOST
    home_on = [jnp.int32(0)] * HOME_MOST
    own_site = [jnp.int32(0)] * OWN_SLOTS
    own_on = [jnp.int32(0)] * OWN_SLOTS
    for k in range(turbines):
        site = site_s[0, k]
        block = block_s[0, k]
        slot = slot_s[0, k]
        for j in range(HOME_MOST):
            hit = site == tile * HOME_MOST + j
            home_slot[j] = jnp.where(hit, slot, home_slot[j])
            home_block[j] = jnp.where(hit, block, home_block[j])
            home_on[j] = jnp.where(hit, 1, home_on[j])
        for j in range(OWN_SLOTS):
            hit = slot == tile * OWN_SLOTS + j
            own_site[j] = jnp.where(hit, site, own_site[j])
            own_on[j] = jnp.where(hit, 1, own_on[j])

    lane = lax.broadcasted_iota(jnp.int32, (ROWS, LANES), 1)
    row_id = lax.broadcasted_iota(jnp.int32, (ROWS, LANES), 0)
    lane_seg = lane // BY
    row_in = row_id % BX
    row_half = row_id // BX

    def stencil_tile(src, dst, xt):
        r = first + xt * ROWS
        here = pl.ds(r, ROWS)
        below_rows = pl.ds(r - 1, ROWS)
        above_rows = pl.ds(r + 1, ROWS)
        for l in range(levels):
            centre = [[q[src, c, l, h, here, :] for h in range(halves)] for c in range(3)]
            rolled_m = [
                [pltpu.roll(centre[c][h], 1, 1) for h in range(halves)] for c in range(3)
            ]
            rolled_p = [
                [pltpu.roll(centre[c][h], LANES - 1, 1) for h in range(halves)]
                for c in range(3)
            ]
            for h in range(halves):
                plus, minus = [], []
                for c in range(3):
                    mid = centre[c][h]
                    xm = q[src, c, l, h, below_rows, :]
                    xp = q[src, c, l, h, above_rows, :]
                    ym = jnp.where(lane == 0, rolled_m[c][h - 1], rolled_m[c][h])
                    yp = jnp.where(
                        lane == LANES - 1, rolled_p[c][(h + 1) % halves], rolled_p[c][h]
                    )
                    zm = mid if l == 0 else q[src, c, l - 1, h, here, :]
                    zp = mid if l == levels - 1 else q[src, c, l + 1, h, here, :]
                    plus.append([xp - mid, yp - mid, zp - mid])
                    minus.append([mid - xm, mid - ym, mid - zm])

                def grad(c, a):
                    return plus[c][a] + minus[c][a]

                gxx, gyy, gzz = grad(0, 0), grad(1, 1), grad(2, 2)
                sxy = grad(0, 1) + grad(1, 0)
                sxz = grad(0, 2) + grad(2, 0)
                syz = grad(1, 2) + grad(2, 1)
                strain = 2.0 * (gxx * gxx + gyy * gyy + gzz * gzz)
                strain = strain + sxy * sxy + sxz * sxz + syz * syz + 4.0 * FLOOR
                nu = (0.5 * SMAG * TIME_STEP) * (strain * lax.rsqrt(strain))
                ups, downs = [], []
                for a in range(3):
                    speed = TIME_STEP * centre[a][h]
                    ups.append(nu - jnp.minimum(speed, 0.0))
                    downs.append(nu + jnp.maximum(speed, 0.0))
                for c in range(3):
                    change = ups[0] * plus[c][0] - downs[0] * minus[c][0]
                    change += ups[1] * plus[c][1] - downs[1] * minus[c][1]
                    change += ups[2] * plus[c][2] - downs[2] * minus[c][2]
                    q[dst, c, l, h, here, :] = centre[c][h] + change

    def unpack_edge(step):
        src = step % 2
        left = pl.ds(first - 1, 1)
        right = pl.ds(first + width_x, 1)

        @pl.when(tile > 0)
        def _():
            edge_copy(step, 1).wait_recv()

        def fill(side, rows, value):
            for c in range(3):
                for l in range(levels):
                    for h in range(halves):
                        q[src, c, l, h, rows, :] = value(c, l, h)

        def received(side):
            return lambda c, l, h: edge_in[
                step, side, pl.ds((c * levels + l) * halves + h, 1), :
            ]

        @pl.when(tile > 0)
        def _():
            fill(0, left, received(0))

        @pl.when(tile == 0)
        def _():
            if step == 0:
                for d in range(1, layouts):
                    pltpu.make_async_remote_copy(
                        src_ref=planes.at[layout],
                        dst_ref=planes.at[layout_at(layouts - d)],
                        send_sem=plane_send.at[d],
                        recv_sem=plane_recv.at[d],
                        device_id=(layout_at(d), tile),
                        device_id_type=MESH,
                    ).wait_recv()
            fill(
                0,
                left,
                lambda c, l, h: planes[step, c, pl.ds(l, 1), pl.ds(h * LANES, LANES)],
            )

        @pl.when(tile < tiles - 1)
        def _():
            edge_copy(step, 0).wait_recv()
            fill(1, right, received(1))

        @pl.when(tile == tiles - 1)
        def _():
            fill(
                1,
                right,
                lambda c, l, h: q[src, c, l, h, pl.ds(first + width_x - 1, 1), :],
            )

    place = []
    for j in range(HOME_MOST):
        xb = lax.div(home_block[j], jnp.int32(y_blocks))
        yb = lax.rem(home_block[j], jnp.int32(y_blocks))
        per = ROWS // BX
        place.append(
            (
                lax.div(xb, jnp.int32(per)),
                lax.rem(xb, jnp.int32(per)),
                lax.div(yb, jnp.int32(segs)),
                lax.rem(yb, jnp.int32(segs)),
            )
        )

    def lay_weights():
        params = []
        for j in range(HOME_MOST):
            owner = lax.div(home_slot[j], jnp.int32(OWN_SLOTS))
            which = lax.rem(home_slot[j], jnp.int32(OWN_SLOTS))
            slab = gathered[0]
            for o in range(1, tiles):
                slab = jnp.where(owner == o, gathered[o], slab)
            rows = slab[:levels]
            param = slab[OWN_SLOTS * levels : OWN_SLOTS * levels + 1]
            for i in range(1, OWN_SLOTS):
                rows = jnp.where(which == i, slab[i * levels : (i + 1) * levels], rows)
                at = OWN_SLOTS * levels + i
                param = jnp.where(which == i, slab[at : at + 1], param)
            rolled = [rows if d == 0 else pltpu.roll(rows, d * BY, 1) for d in range(segs)]
            _, x_half, _, seg = place[j]
            inside = (row_half == x_half) & (lane_seg == seg) & (home_on[j] > 0)
            for l in range(levels):
                laid = jnp.zeros((ROWS, LANES), jnp.float32)
                for d in range(segs):
                    spread = jnp.broadcast_to(rolled[d][l : l + 1, :], (ROWS, LANES))
                    pick = lax.rem(lane_seg - row_in + segs, segs) == d
                    laid = jnp.where(pick, spread, laid)
                weights_v[j, l] = jnp.where(inside, laid, 0.0)
            params.append([param[:, i : i + 1] for i in range(4)])
        return params

    def disk(src, params):
        found = [[[None] * levels for _ in range(2)] for _ in range(HOME_MOST)]
        for xt in range(x_tiles):
            rows = pl.ds(first + xt * ROWS, ROWS)
            for h in range(halves):
                on = [(place[j][0] == xt) & (place[j][2] == h) for j in range(HOME_MOST)]
                for c in range(2):
                    for l in range(levels):
                        cells = q[src, c, l, h, rows, :]
                        for j in range(HOME_MOST):
                            old = found[j][c][l]
                            found[j][c][l] = (
                                cells if old is None else jnp.where(on[j], cells, old)
                            )
        results = []
        for j in range(HOME_MOST):
            cosine, sine, coef, inverse = params[j]
            acc_u = jnp.zeros((ROWS, LANES), jnp.float32)
            acc_v = jnp.zeros((ROWS, LANES), jnp.float32)
            for l in range(levels):
                w = weights_v[j, l]
                acc_u += w * found[j][0][l]
                acc_v += w * found[j][1][l]
            normal = acc_u * cosine + acc_v * sine
            total = jnp.sum(jnp.sum(normal, axis=0, keepdims=True), axis=1, keepdims=True)
            speed = total * inverse
            pull = 0.5 * coef * jnp.abs(speed) * speed
            push = -TIME_STEP * pull
            results.append((push * cosine, push * sine, pull * speed))
        return results

    def add_force(dst, results):
        for xt in range(x_tiles):
            rows = pl.ds(first + xt * ROWS, ROWS)
            for h in range(halves):
                scale = []
                for j in range(HOME_MOST):
                    on = (place[j][0] == xt) & (place[j][2] == h)
                    scale.append([jnp.where(on, results[j][c], 0.0) for c in range(2)])
                for l in range(levels):
                    w = [weights_v[j, l] for j in range(HOME_MOST)]
                    for c in range(2):
                        force = scale[0][c] * w[0]
                        for j in range(1, HOME_MOST):
                            force += scale[j][c] * w[j]
                        q[dst, c, l, h, rows, :] += force

    def power_copy(d):
        return pltpu.make_async_remote_copy(
            src_ref=powers.at[tile],
            dst_ref=powers.at[tile],
            send_sem=power_send.at[d],
            recv_sem=power_recv.at[d],
            device_id=(layout, tile_at(d)),
            device_id_type=MESH,
        )

    power_row = jnp.zeros((1, LANES), jnp.float32)
    params = None
    for step in range(steps):
        src, dst = step % 2, (step + 1) % 2
        results = None
        if step > 0:
            results = disk(src, params)
        if step > 0 and step == steps - 1:
            for j in range(HOME_MOST):
                power_row = power_row + jnp.where(lane1 == j, results[j][2], 0.0)
            powers[tile] = power_row * (1.0 / steps)
            for d in range(1, tiles):
                power_copy(d).start()
        lax.fori_loop(
            1, x_tiles - 1, lambda xt, c: (stencil_tile(src, dst, xt), c)[1], 0
        )
        unpack_edge(step)
        lax.fori_loop(
            0,
            2,
            lambda i, c: (stencil_tile(src, dst, i * (x_tiles - 1)), c)[1],
            0,
        )
        if step == 0:
            for d in range(1, tiles):
                pltpu.make_async_remote_copy(
                    src_ref=gathered.at[tile],
                    dst_ref=gathered.at[tile_at(tiles - d)],
                    send_sem=gather_send.at[d],
                    recv_sem=gather_recv.at[d],
                    device_id=(layout, tile_at(d)),
                    device_id_type=MESH,
                ).wait_recv()
            params = lay_weights()
            results = disk(src, params)
        add_force(dst, results)
        if step < steps - 1:
            for j in range(HOME_MOST):
                power_row = power_row + jnp.where(lane1 == j, results[j][2], 0.0)
            pack_edge(step + 1, 0)
            pack_edge(step + 1, 1)
            send_edges(step + 1)

    final = steps % 2
    stores = [
        pltpu.make_async_copy(
            q.at[final, :, :, h, pl.ds(first, width_x), :],
            out_ref.at[0, :, :, :, pl.ds(h * LANES, LANES)],
            local_sem.at[3 + h],
        )
        for h in range(halves)
    ]
    for copy in stores:
        copy.start()

    for d in range(1, tiles):
        pltpu.make_async_remote_copy(
            src_ref=powers.at[tile],
            dst_ref=powers.at[tile_at(tiles - d)],
            send_sem=power_send.at[d],
            recv_sem=power_recv.at[d],
            device_id=(layout, tile_at(d)),
            device_id_type=MESH,
        ).wait_recv()
    lane_out = lax.broadcasted_iota(jnp.int32, (1, OWN_SLOTS), 1)
    answer = jnp.zeros((1, OWN_SLOTS), jnp.float32)
    rows_in = [powers[o] for o in range(tiles)]
    for j in range(OWN_SLOTS):
        home = lax.div(own_site[j], jnp.int32(HOME_MOST))
        which = lax.rem(own_site[j], jnp.int32(HOME_MOST))
        row = rows_in[0]
        for o in range(1, tiles):
            row = jnp.where(home == o, rows_in[o], row)
        value = jnp.sum(jnp.where(lane1 == which, row, 0.0), axis=1, keepdims=True)
        value = jnp.where(own_on[j] > 0, value, 0.0)
        answer = jnp.where(lane_out == j, value, answer)
    power_v[...] = answer
    last = pltpu.make_async_copy(power_v, power_ref, local_sem.at[0])
    last.start()

    for step in range(steps):
        @pl.when(tile > 0)
        def _():
            edge_copy(step, 0).wait_send()

        @pl.when(tile < tiles - 1)
        def _():
            edge_copy(step, 1).wait_send()

    @pl.when(tile == 0)
    def _():
        for d in range(1, layouts):
            plane_copy(d).wait_send()

    for d in range(1, tiles):
        gather_copy(d).wait_send()
        power_copy(d).wait_send()
    last.wait()
    for copy in stores:
        copy.wait()


def solution(mesh):
    tiles = mesh.shape["tile"]
    layouts = mesh.shape["layout"]

    def local(velocity, inflow, turbine_site, turbine_block, turbine_slot, smear, yaw, thrust_coef):
        _, _, levels, width_x, width_y = velocity.shape
        halves = width_y // LANES
        turbines = turbine_site.shape[1]
        edge_rows = 3 * levels * halves
        f32 = jnp.float32
        slab = -(-OWN_SLOTS * (levels + 1) // ROWS) * ROWS
        dma = pltpu.SemaphoreType.DMA
        anywhere = pl.BlockSpec(memory_space=pl.ANY)
        return pl.pallas_call(
            functools.partial(kernel, tiles, layouts, levels, width_x, halves, turbines),
            out_shape=(
                jax.ShapeDtypeStruct(velocity.shape, f32),
                jax.ShapeDtypeStruct(yaw.shape, f32),
            ),
            in_specs=[anywhere] * 8,
            out_specs=(anywhere, anywhere),
            scratch_shapes=[
                pltpu.VMEM((2, 3, levels, halves, width_x + 2 * ROWS, LANES), f32),
                pltpu.SMEM((1, turbines), jnp.int32),
                pltpu.SMEM((1, turbines), jnp.int32),
                pltpu.SMEM((1, turbines), jnp.int32),
                pltpu.VMEM(smear.shape[1:], f32),
                pltpu.VMEM(yaw.shape, f32),
                pltpu.VMEM(yaw.shape, f32),
                pltpu.VMEM((tiles, slab, LANES), f32),
                pltpu.VMEM((HOME_MOST, levels, ROWS, LANES), f32),
                pltpu.VMEM((layouts, 3, levels, width_y), f32),
                pltpu.VMEM((layouts, 2, edge_rows, LANES), f32),
                pltpu.VMEM((layouts, 2, edge_rows, LANES), f32),
                pltpu.VMEM((tiles, 1, LANES), f32),
                pltpu.VMEM((1, OWN_SLOTS), f32),
                dma((7 + halves,)),
                dma((tiles,)),
                dma((tiles,)),
                dma((layouts,)),
                dma((layouts,)),
                dma((layouts, 2)),
                dma((layouts, 2)),
                dma((tiles,)),
                dma((tiles,)),
            ],
            compiler_params=pltpu.CompilerParams(
                collective_id=0, has_side_effects=True, vmem_limit_bytes=24 * 1024 * 1024
            ),
        )(velocity, inflow, turbine_site, turbine_block, turbine_slot, smear, yaw, thrust_coef)

    in_specs = (
        P("layout", None, None, "tile", None),
        P("layout", None, None, None),
        P("layout", None),
        P("layout", None),
        P("layout", None),
        P("layout", "tile", None),
        P("layout", "tile"),
        P("layout", "tile"),
    )
    out_specs = (P("layout", None, None, "tile", None), P("layout", "tile"))
    return jax.shard_map(local, mesh=mesh, in_specs=in_specs, out_specs=out_specs, check_vma=False)
```

time: 162 us -> 21.6 us (0.13)
  blocking collectives: 89 us -> 0 us
  local copies, waits for them, and re-layouts: 42.1 us -> 3.65 us
  Pallas kernels: 0 us -> 17 us
  between operations: 12.2 us -> 0.71 us
  other arithmetic: 9.35 us -> 0 us
  starting transfers between devices: 5.33 us -> 0 us
  matrix products: 2.63 us -> 0 us
    all_gather x4 -> x0, blocking collectives: 79.6 us -> none  [the longest x2 43.4 us: local(): lax.all_gather(disk_blocks, 'tile', axis=0, tiled=True)]
    pallas_call x0 -> x1, Pallas kernels: none -> 17 us  [local(): pl.pallas_call(functools.partial(kernel, tiles, layouts, levels, width_x,...]
    dynamic_update_slice x6 -> x0, local copies, waits for them, and re-layouts: 16 us -> none  [local(): lax.dynamic_update_slice(spread, existing + home_force[slot_index].reshap...]
    psum x1 -> x0, blocking collectives: 9.34 us -> none  [from_root(): return lax.psum(jnp.where(mine, shard, jnp.zeros_like(shard)), axis)]
    gather x4 -> x0, local copies, waits for them, and re-layouts: 9.3 us -> none  [take_one(): lax.dynamic_slice(source, (zero_index, zero_index, x_first, y_first), (2,...]
    add x1 -> x0, local copies, waits for them, and re-layouts: 5.88 us -> none  [local(): stepped[:2] + time_step * spread]
    ppermute x4 -> x0, starting transfers between devices: 5.33 us -> none  [the longest x2 2.76 us: extended(): before = lax.ppermute(last, axis, up)]
    slice x14 -> x0, local copies, waits for them, and re-layouts: 3.51 us -> none  [the longest x1 0.97 us: local(): source = current[:2]]
  transfers between devices with their start and end apart: 4 -> 0, of which waited for: 0 -> 0; matrix products, arithmetic and copies ran while one was open for 21% -> 0% of each run, Pallas kernels for 0% -> 0%
where the time goes in v1:
time: 21.6 us; the launch traced here: 21.4 us
  Pallas kernels  17 us (79%)
  local copies, waits for them, and re-layouts  3.65 us (17%)
  between operations  0.71 us (3%)
    pallas_call x1, Pallas kernels, local(): pl.pallas_call(functools.partial(kernel, tiles, layouts, levels, width_x,...  17 us
    unnamed x17, local copies, waits for them, and re-layouts  3.65 us

profile of v1, /device:TPU:0, one launch (start us, length us, event | category | flops | bytes accessed | tf_op | source)
XLA Modules:
  0.0 21.4 jit_solution(12618667077488437366)
XLA Ops:
  0.6 0.0 copy-start.5
  0.6 0.0 copy-start.4
  0.7 0.0 copy-start.3
  0.7 0.0 copy-start.2
  0.7 0.0 copy-start.1
  0.7 0.7 %copy.10.smear_ref = f32[1,3,512]{2,1,0:T(4,128)S(1)} copy(f32[1,3,512]{2,0,1:T(1,128)} %param.13) | data formatting | bytes 12288 | tf_op args[5]
  1.4 0.0 copy-done.5
  1.4 0.0 copy-done.4
  1.4 0.0 copy-done.3
  1.4 0.0 copy-done.2
  1.4 0.0 copy-done.1
  1.4 0.0 copy-start
  1.4 1.0 %copy-done = f32[1,3,4,32,256]{4,3,2,1,0:T(8,128)S(1)} copy-done((f32[1,3,4,32,256]{4,3,2,1,0:T(8,128)S(1)}, f32[1,3,4,32,256]{4,3,2,1,0:T(8,128)}, u32[]{:S(2)}) %copy-start) | copy-done | bytes 393240
  2.4 0.0 copy-start.6
  2.4 0.7 %copy-done.6 = f32[1,3]{1,0:T(1,128)S(1)} copy-done((f32[1,3]{1,0:T(1,128)S(1)}, f32[1,3]{1,0:T(1,128)}, u32[]{:S(2)}) %copy-start.6) | copy-done | bytes 36
  3.1 17.0 %shard_map.95 = (f32[1,3,4,32,256]{4,3,2,1,0:T(8,128)S(1)}, f32[1,3]{1,0:T(1,128)S(1)}) custom-call(f32[1,3,4,32,256]{4,3,2,1,0:T(8,128)S(1)} %copy-done, f32[1,3,4,256]{3,2,1,0:T(4,128)S(1)} %copy-done.1, s32[1,40]{1,0:T(1,128)S(1)} %copy-done.2, s32[1,40]{1,0:T(1,128)S(1)} %copy-done.3, s32[1,40]{1,0:T(1,128)S(1)} %copy-done.4, ...), custom_call_target="tpu_custom_call" | custom-call | tf_op jit(solution)/shard_map/pallas_call | solution.py:513
  20.1 0.7 %copy.13 = f32[1,3,4,32,256]{4,3,2,1,0:T(8,128)} copy(f32[1,3,4,32,256]{4,3,2,1,0:T(8,128)S(1)} %get-tuple-element.4) | data formatting | bytes 786432
  20.9 0.5 %copy.14 = f32[1,3]{1,0:T(1,128)} copy(f32[1,3]{1,0:T(1,128)S(1)} %get-tuple-element.5) | data formatting | bytes 24
Async XLA Ops:
  0.6 0.8 %copy-start.5 = (f32[1,3]{1,0:T(1,128)S(1)}, f32[1,3]{1,0:T(1,128)}, u32[]{:S(2)}) copy-start(f32[1,3]{1,0:T(1,128)} %yaw_ref.1) | copy-start | bytes 40
  0.6 0.8 %copy-start.4 = (s32[1,40]{1,0:T(1,128)S(1)}, s32[1,40]{1,0:T(1,128)}, u32[]{:S(2)}) copy-start(s32[1,40]{1,0:T(1,128)} %slot_ref.1) | copy-start | bytes 484
  0.7 0.8 %copy-start.3 = (s32[1,40]{1,0:T(1,128)S(1)}, s32[1,40]{1,0:T(1,128)}, u32[]{:S(2)}) copy-start(s32[1,40]{1,0:T(1,128)} %block_ref.1) | copy-start | bytes 484
  0.7 0.8 %copy-start.2 = (s32[1,40]{1,0:T(1,128)S(1)}, s32[1,40]{1,0:T(1,128)}, u32[]{:S(2)}) copy-start(s32[1,40]{1,0:T(1,128)} %site_ref.1) | copy-start | bytes 484
  0.7 0.8 %copy-start.1 = (f32[1,3,4,256]{3,2,1,0:T(4,128)S(1)}, f32[1,3,4,256]{3,2,1,0:T(4,128)}, u32[]{:S(2)}) copy-start(f32[1,3,4,256]{3,2,1,0:T(4,128)} %inflow_ref.1) | copy-start | bytes 36868
  1.4 1.0 %copy-start = (f32[1,3,4,32,256]{4,3,2,1,0:T(8,128)S(1)}, f32[1,3,4,32,256]{4,3,2,1,0:T(8,128)}, u32[]{:S(2)}) copy-start(f32[1,3,4,32,256]{4,3,2,1,0:T(8,128)} %vel_ref.1) | copy-start | bytes 1179652
  2.4 0.7 %copy-start.6 = (f32[1,3]{1,0:T(1,128)S(1)}, f32[1,3]{1,0:T(1,128)}, u32[]{:S(2)}) copy-start(f32[1,3]{1,0:T(1,128)} %coef_ref.1) | copy-start | bytes 40

commit v2 on v1

--- a/solution.py
+++ b/solution.py
@@ -26,7 +26,7 @@
     vel_ref, inflow_ref, site_ref, block_ref, slot_ref, smear_ref, yaw_ref, coef_ref,
     out_ref, power_ref,
     q, site_s, block_s, slot_s, smear_v, yaw_v, coef_v, gathered, weights_v,
-    planes, edge_out, edge_in, powers, power_v,
+    planes, edge_out, edge_in, powers,
     local_sem, gather_send, gather_recv, plane_send, plane_recv,
     edge_send, edge_recv, power_send, power_recv,
 ):
@@ -56,7 +56,7 @@
         )
 
     loads = [
-        pltpu.make_async_copy(smear_ref.at[0], smear_v, local_sem.at[0]),
+        pltpu.make_async_copy(smear_ref.at[:, 0], smear_v, local_sem.at[0]),
         pltpu.make_async_copy(yaw_ref, yaw_v, local_sem.at[1]),
         pltpu.make_async_copy(coef_ref, coef_v, local_sem.at[2]),
     ]
@@ -192,7 +192,7 @@
     row_in = row_id % BX
     row_half = row_id // BX
 
-    def stencil_tile(src, dst, xt):
+    def stencil_tile(src, put, xt):
         r = first + xt * ROWS
         here = pl.ds(r, ROWS)
         below_rows = pl.ds(r - 1, ROWS)
@@ -240,7 +240,7 @@
                     change = ups[0] * plus[c][0] - downs[0] * minus[c][0]
                     change += ups[1] * plus[c][1] - downs[1] * minus[c][1]
                     change += ups[2] * plus[c][2] - downs[2] * minus[c][2]
-                    q[dst, c, l, h, here, :] = centre[c][h] + change
+                    put(c, l, h, xt, centre[c][h] + change)
 
     def unpack_edge(step):
         src = step % 2
@@ -369,9 +369,8 @@
             results.append((push * cosine, push * sine, pull * speed))
         return results
 
-    def add_force(dst, results):
+    def add_force(get, put, results):
         for xt in range(x_tiles):
-            rows = pl.ds(first + xt * ROWS, ROWS)
             for h in range(halves):
                 scale = []
                 for j in range(HOME_MOST):
@@ -383,7 +382,7 @@
                         force = scale[0][c] * w[0]
                         for j in range(1, HOME_MOST):
                             force += scale[j][c] * w[j]
-                        q[dst, c, l, h, rows, :] += force
+                        put(c, l, h, xt, get(c, l, h, xt) + force)
 
     def power_copy(d):
         return pltpu.make_async_remote_copy(
@@ -395,10 +394,29 @@
             device_id_type=MESH,
         )
 
+    def access(step):
+        dst = (step + 1) % 2
+
+        def where_at(c, l, h, xt):
+            if step == steps - 1:
+                return out_ref, (0, c, l, pl.ds(xt * ROWS, ROWS), pl.ds(h * LANES, LANES))
+            return q, (dst, c, l, h, pl.ds(first + xt * ROWS, ROWS), slice(None))
+
+        def get(*at):
+            ref, index = where_at(*at)
+            return ref[index]
+
+        def put(c, l, h, xt, value):
+            ref, index = where_at(c, l, h, xt)
+            ref[index] = value
+
+        return get, put
+
     power_row = jnp.zeros((1, LANES), jnp.float32)
     params = None
     for step in range(steps):
         src, dst = step % 2, (step + 1) % 2
+        get, put = access(step)
         results = None
         if step > 0:
             results = disk(src, params)
@@ -409,13 +427,13 @@
             for d in range(1, tiles):
                 power_copy(d).start()
         lax.fori_loop(
-            1, x_tiles - 1, lambda xt, c: (stencil_tile(src, dst, xt), c)[1], 0
+            1, x_tiles - 1, lambda xt, c: (stencil_tile(src, put, xt), c)[1], 0
         )
         unpack_edge(step)
         lax.fori_loop(
             0,
             2,
-            lambda i, c: (stencil_tile(src, dst, i * (x_tiles - 1)), c)[1],
+            lambda i, c: (stencil_tile(src, put, i * (x_tiles - 1)), c)[1],
             0,
         )
         if step == 0:
@@ -430,25 +448,13 @@
                 ).wait_recv()
             params = lay_weights()
             results = disk(src, params)
-        add_force(dst, results)
+        add_force(get, put, results)
         if step < steps - 1:
             for j in range(HOME_MOST):
                 power_row = power_row + jnp.where(lane1 == j, results[j][2], 0.0)
             pack_edge(step + 1, 0)
             pack_edge(step + 1, 1)
             send_edges(step + 1)
-
-    final = steps % 2
-    stores = [
-        pltpu.make_async_copy(
-            q.at[final, :, :, h, pl.ds(first, width_x), :],
-            out_ref.at[0, :, :, :, pl.ds(h * LANES, LANES)],
-            local_sem.at[3 + h],
-        )
-        for h in range(halves)
-    ]
-    for copy in stores:
-        copy.start()
 
     for d in range(1, tiles):
         pltpu.make_async_remote_copy(
@@ -471,9 +477,7 @@
         value = jnp.sum(jnp.where(lane1 == which, row, 0.0), axis=1, keepdims=True)
         value = jnp.where(own_on[j] > 0, value, 0.0)
         answer = jnp.where(lane_out == j, value, answer)
-    power_v[...] = answer
-    last = pltpu.make_async_copy(power_v, power_ref, local_sem.at[0])
-    last.start()
+    power_ref[...] = answer
 
     for step in range(steps):
         @pl.when(tile > 0)
@@ -492,9 +496,6 @@
     for d in range(1, tiles):
         gather_copy(d).wait_send()
         power_copy(d).wait_send()
-    last.wait()
-    for copy in stores:
-        copy.wait()
 
 
 def solution(mesh):
@@ -509,15 +510,15 @@
         f32 = jnp.float32
         slab = -(-OWN_SLOTS * (levels + 1) // ROWS) * ROWS
         dma = pltpu.SemaphoreType.DMA
-        anywhere = pl.BlockSpec(memory_space=pl.ANY)
+        inside = pl.BlockSpec(memory_space=pltpu.VMEM)
         return pl.pallas_call(
             functools.partial(kernel, tiles, layouts, levels, width_x, halves, turbines),
             out_shape=(
-                jax.ShapeDtypeStruct(velocity.shape, f32),
-                jax.ShapeDtypeStruct(yaw.shape, f32),
+                pltpu.VMEM(velocity.shape, f32),
+                pltpu.VMEM(yaw.shape, f32),
             ),
-            in_specs=[anywhere] * 8,
-            out_specs=(anywhere, anywhere),
+            in_specs=[pl.BlockSpec(memory_space=pltpu.HBM)] * 8,
+            out_specs=(inside, inside),
             scratch_shapes=[
                 pltpu.VMEM((2, 3, levels, halves, width_x + 2 * ROWS, LANES), f32),
                 pltpu.SMEM((1, turbines), jnp.int32),
@@ -532,7 +533,6 @@
                 pltpu.VMEM((layouts, 2, edge_rows, LANES), f32),
                 pltpu.VMEM((layouts, 2, edge_rows, LANES), f32),
                 pltpu.VMEM((tiles, 1, LANES), f32),
-                pltpu.VMEM((1, OWN_SLOTS), f32),
                 dma((7 + halves,)),
                 dma((tiles,)),
                 dma((tiles,)),
@@ -546,7 +546,10 @@
             compiler_params=pltpu.CompilerParams(
                 collective_id=0, has_side_effects=True, vmem_limit_bytes=24 * 1024 * 1024
             ),
-        )(velocity, inflow, turbine_site, turbine_block, turbine_slot, smear, yaw, thrust_coef)
+        )(
+            velocity, inflow, turbine_site, turbine_block, turbine_slot,
+            jnp.transpose(smear, (1, 0, 2)), yaw, thrust_coef,
+        )
 
     in_specs = (
         P("layout", None, None, "tile", None),

time: 21.6 us -> 23.6 us (1.093)
  local copies, waits for them, and re-layouts: 3.65 us -> 5.62 us
    unnamed x17 -> x18, local copies, waits for them, and re-layouts: 3.65 us -> 5.62 us
where the time goes in v2:
time: 23.6 us; the launch traced here: 23.3 us
  Pallas kernels  17 us (72%)
  local copies, waits for them, and re-layouts  5.62 us (24%)
  between operations  0.67 us (3%)
    pallas_call x1, Pallas kernels, local(): pl.pallas_call(functools.partial(kernel, tiles, layouts, levels, width_x,...  17 us
    unnamed x18, local copies, waits for them, and re-layouts  5.62 us

profile of v2, /device:TPU:0, one launch (start us, length us, event | category | flops | bytes accessed | tf_op | source)
XLA Modules:
  0.0 23.3 jit_solution(9327645989521895412)
XLA Ops:
  0.6 0.0 copy-start.5
  0.6 0.0 copy-start.4
  0.7 0.0 copy-start.3
  0.7 0.6 %copy-done.5 = s32[1,40]{1,0:T(1,128)S(1)} copy-done((s32[1,40]{1,0:T(1,128)S(1)}, s32[1,40]{1,0:T(1,128)}, u32[]{:S(2)}) %copy-start.5) | copy-done | bytes 184
  1.3 0.0 copy-done.4
  1.3 0.0 copy-done.3
  1.3 0.0 copy-start
  1.3 1.0 %copy-done = f32[1,3,4,32,256]{4,3,2,1,0:T(8,128)S(1)} copy-done((f32[1,3,4,32,256]{4,3,2,1,0:T(8,128)S(1)}, f32[1,3,4,32,256]{4,3,2,1,0:T(8,128)}, u32[]{:S(2)}) %copy-start) | copy-done | bytes 393240
  2.3 0.0 copy-start.1
  2.3 0.7 %copy-done.1 = f32[1,3,4,256]{3,2,1,0:T(4,128)S(1)} copy-done((f32[1,3,4,256]{3,2,1,0:T(4,128)S(1)}, f32[1,3,4,256]{3,2,1,0:T(4,128)}, u32[]{:S(2)}) %copy-start.1) | copy-done | bytes 12312
  3.0 0.0 copy-start.2
  3.0 0.7 %copy-done.2 = f32[1,3,512]{2,0,1:T(1,128)S(1)} copy-done((f32[1,3,512]{2,0,1:T(1,128)S(1)}, f32[1,3,512]{2,0,1:T(1,128)}, u32[]{:S(2)}) %copy-start.2) | copy-done | bytes 6168
  3.7 0.0 copy-start.6
  3.7 0.7 %copy-done.6 = f32[1,3]{1,0:T(1,128)S(1)} copy-done((f32[1,3]{1,0:T(1,128)S(1)}, f32[1,3]{1,0:T(1,128)}, u32[]{:S(2)}) %copy-start.6) | copy-done | bytes 36
  4.4 0.0 copy-start.7
  4.4 0.7 %copy-done.7 = f32[1,3]{1,0:T(1,128)S(1)} copy-done((f32[1,3]{1,0:T(1,128)S(1)}, f32[1,3]{1,0:T(1,128)}, u32[]{:S(2)}) %copy-start.7) | copy-done | bytes 36
  5.0 17.0 %shard_map.95 = (f32[1,3,4,32,256]{4,3,2,1,0:T(8,128)S(1)}, f32[1,3]{1,0:T(1,128)S(1)}) custom-call(f32[1,3,4,32,256]{4,3,2,1,0:T(8,128)S(1)} %copy-done, f32[1,3,4,256]{3,2,1,0:T(4,128)S(1)} %copy-done.1, s32[1,40]{1,0:T(1,128)S(1)} %copy-done.3, s32[1,40]{1,0:T(1,128)S(1)} %copy-done.4, s32[1,40]{1,0:T(1,128)S(1)} %copy-done.5, f32[3,1,512]{2,1,0:T(1,128)S(1)} %bitcast.1, ...), custom_call_target="tpu_custom_call" | custom-call | tf_op jit(solution)/shard_map/pallas_call | solution.py:514
  22.0 0.7 %copy.12 = f32[1,3,4,32,256]{4,3,2,1,0:T(8,128)} copy(f32[1,3,4,32,256]{4,3,2,1,0:T(8,128)S(1)} %get-tuple-element.2) | data formatting | bytes 786432
  22.8 0.5 %copy.13 = f32[1,3]{1,0:T(1,128)} copy(f32[1,3]{1,0:T(1,128)S(1)} %get-tuple-element.3) | data formatting | bytes 24
Async XLA Ops:
  0.6 0.7 %copy-start.5 = (s32[1,40]{1,0:T(1,128)S(1)}, s32[1,40]{1,0:T(1,128)}, u32[]{:S(2)}) copy-start(s32[1,40]{1,0:T(1,128)} %slot_ref.1) | copy-start | bytes 484
  0.6 0.7 %copy-start.4 = (s32[1,40]{1,0:T(1,128)S(1)}, s32[1,40]{1,0:T(1,128)}, u32[]{:S(2)}) copy-start(s32[1,40]{1,0:T(1,128)} %block_ref.1) | copy-start | bytes 484
  0.7 0.7 %copy-start.3 = (s32[1,40]{1,0:T(1,128)S(1)}, s32[1,40]{1,0:T(1,128)}, u32[]{:S(2)}) copy-start(s32[1,40]{1,0:T(1,128)} %site_ref.1) | copy-start | bytes 484
  1.3 1.0 %copy-start = (f32[1,3,4,32,256]{4,3,2,1,0:T(8,128)S(1)}, f32[1,3,4,32,256]{4,3,2,1,0:T(8,128)}, u32[]{:S(2)}) copy-start(f32[1,3,4,32,256]{4,3,2,1,0:T(8,128)} %vel_ref.1) | copy-start | bytes 1179652
  2.3 0.7 %copy-start.1 = (f32[1,3,4,256]{3,2,1,0:T(4,128)S(1)}, f32[1,3,4,256]{3,2,1,0:T(4,128)}, u32[]{:S(2)}) copy-start(f32[1,3,4,256]{3,2,1,0:T(4,128)} %inflow_ref.1) | copy-start | bytes 36868
  3.0 0.7 %copy-start.2 = (f32[1,3,512]{2,0,1:T(1,128)S(1)}, f32[1,3,512]{2,0,1:T(1,128)}, u32[]{:S(2)}) copy-start(f32[1,3,512]{2,0,1:T(1,128)} %param.13) | copy-start | bytes 18436
  3.7 0.7 %copy-start.6 = (f32[1,3]{1,0:T(1,128)S(1)}, f32[1,3]{1,0:T(1,128)}, u32[]{:S(2)}) copy-start(f32[1,3]{1,0:T(1,128)} %yaw_ref.1) | copy-start | bytes 40
  4.4 0.7 %copy-start.7 = (f32[1,3]{1,0:T(1,128)S(1)}, f32[1,3]{1,0:T(1,128)}, u32[]{:S(2)}) copy-start(f32[1,3]{1,0:T(1,128)} %coef_ref.1) | copy-start | bytes 40

commit v3 on v2

--- a/solution.py
+++ b/solution.py
@@ -544,7 +544,7 @@
                 dma((tiles,)),
             ],
             compiler_params=pltpu.CompilerParams(
-                collective_id=0, has_side_effects=True, vmem_limit_bytes=24 * 1024 * 1024
+                collective_id=0, has_side_effects=True, vmem_limit_bytes=60 * 1024 * 1024
             ),
         )(
             velocity, inflow, turbine_site, turbine_block, turbine_slot,

time: 23.6 us -> 19.1 us (0.81)
  local copies, waits for them, and re-layouts: 5.62 us -> 1.26 us
    unnamed x18 -> x2, local copies, waits for them, and re-layouts: 5.62 us -> 1.26 us
where the time goes in v3:
time: 19.1 us; the launch traced here: 19 us
  Pallas kernels  17.1 us (90%)
  local copies, waits for them, and re-layouts  1.26 us (7%)
  between operations  0.64 us (3%)
    pallas_call x1, Pallas kernels, local(): pl.pallas_call(functools.partial(kernel, tiles, layouts, levels, width_x,...  17.1 us
    unnamed x2, local copies, waits for them, and re-layouts  1.26 us

profile of v3, /device:TPU:0, one launch (start us, length us, event | category | flops | bytes accessed | tf_op | source)
XLA Modules:
  0.0 19.0 jit_solution(13964164461406994330)
XLA Ops:
  0.6 17.1 %shard_map.95 = (f32[1,3,4,32,256]{4,3,2,1,0:T(8,128)S(1)}, f32[1,3]{1,0:T(1,128)S(1)}) custom-call(f32[1,3,4,32,256]{4,3,2,1,0:T(8,128)} %vel_ref.1, f32[1,3,4,256]{3,2,1,0:T(4,128)} %inflow_ref.1, s32[1,40]{1,0:T(1,128)} %site_ref.1, s32[1,40]{1,0:T(1,128)} %block_ref.1, s32[1,40]{1,0:T(1,128)} %slot_ref.1, f32[3,1,512]{2,1,0:T(1,128)} %bitcast.1, ...), custom_call_target="tpu_custom_call" | custom-call | tf_op jit(solution)/shard_map/pallas_call | solution.py:514
  17.7 0.7 %copy.12 = f32[1,3,4,32,256]{4,3,2,1,0:T(8,128)} copy(f32[1,3,4,32,256]{4,3,2,1,0:T(8,128)S(1)} %get-tuple-element.2) | data formatting | bytes 786432
  18.4 0.5 %copy.13 = f32[1,3]{1,0:T(1,128)} copy(f32[1,3]{1,0:T(1,128)S(1)} %get-tuple-element.3) | data formatting | bytes 24

commit v4 on v3

--- a/solution.py
+++ b/solution.py
@@ -96,9 +96,6 @@
         packed = jnp.where(lane1 == 3, 1.0 / total, packed)
         gathered[tile, pl.ds(OWN_SLOTS * levels + j, 1), :] = packed
 
-    for copy in field_loads:
-        copy.wait()
-
     def pack_edge(step, side):
         row = first if side == 0 else first + width_x - 1
         for c in range(3):
@@ -129,13 +126,27 @@
         def _():
             edge_copy(step, 1).start()
 
+    pl.semaphore_wait(barrier, tiles - 1 + layouts - 1)
+
+    def gather_copy(d):
+        return pltpu.make_async_remote_copy(
+            src_ref=gathered.at[tile],
+            dst_ref=gathered.at[tile],
+            send_sem=gather_send.at[d],
+            recv_sem=gather_recv.at[d],
+            device_id=(layout, tile_at(d)),
+            device_id_type=MESH,
+        )
+
+    for d in range(1, tiles):
+        gather_copy(d).start()
+
+    for copy in field_loads:
+        copy.wait()
     pack_edge(0, 0)
     pack_edge(0, 1)
+    send_edges(0)
     plane_load.wait()
-
-    pl.semaphore_wait(barrier, tiles - 1 + layouts - 1)
-
-    send_edges(0)
 
     def plane_copy(d):
         return pltpu.make_async_remote_copy(
@@ -151,19 +162,6 @@
     def _():
         for d in range(1, layouts):
             plane_copy(d).start()
-
-    def gather_copy(d):
-        return pltpu.make_async_remote_copy(
-            src_ref=gathered.at[tile],
-            dst_ref=gathered.at[tile],
-            send_sem=gather_send.at[d],
-            recv_sem=gather_recv.at[d],
-            device_id=(layout, tile_at(d)),
-            device_id_type=MESH,
-        )
-
-    for d in range(1, tiles):
-        gather_copy(d).start()
 
     for copy in list_loads:
         copy.wait()
@@ -311,6 +309,9 @@
             )
         )
 
+    def total_of(cells):
+        return jnp.sum(jnp.sum(cells, axis=0, keepdims=True), axis=1, keepdims=True)
+
     def lay_weights():
         params = []
         for j in range(HOME_MOST):
@@ -328,49 +329,57 @@
             rolled = [rows if d == 0 else pltpu.roll(rows, d * BY, 1) for d in range(segs)]
             _, x_half, _, seg = place[j]
             inside = (row_half == x_half) & (lane_seg == seg) & (home_on[j] > 0)
+            square = jnp.zeros((ROWS, LANES), jnp.float32)
             for l in range(levels):
                 laid = jnp.zeros((ROWS, LANES), jnp.float32)
                 for d in range(segs):
                     spread = jnp.broadcast_to(rolled[d][l : l + 1, :], (ROWS, LANES))
                     pick = lax.rem(lane_seg - row_in + segs, segs) == d
                     laid = jnp.where(pick, spread, laid)
-                weights_v[j, l] = jnp.where(inside, laid, 0.0)
-            params.append([param[:, i : i + 1] for i in range(4)])
+                laid = jnp.where(inside, laid, 0.0)
+                weights_v[j, l] = laid
+                square += laid * laid
+            params.append([param[:, i : i + 1] for i in range(4)] + [total_of(square)])
         return params
 
-    def disk(src, params):
+    def disk(read, params):
         found = [[[None] * levels for _ in range(2)] for _ in range(HOME_MOST)]
         for xt in range(x_tiles):
-            rows = pl.ds(first + xt * ROWS, ROWS)
             for h in range(halves):
                 on = [(place[j][0] == xt) & (place[j][2] == h) for j in range(HOME_MOST)]
                 for c in range(2):
                     for l in range(levels):
-                        cells = q[src, c, l, h, rows, :]
+                        cells = read(c, l, h, xt)
                         for j in range(HOME_MOST):
                             old = found[j][c][l]
                             found[j][c][l] = (
                                 cells if old is None else jnp.where(on[j], cells, old)
                             )
-        results = []
+        totals = []
         for j in range(HOME_MOST):
-            cosine, sine, coef, inverse = params[j]
+            cosine, sine = params[j][:2]
             acc_u = jnp.zeros((ROWS, LANES), jnp.float32)
             acc_v = jnp.zeros((ROWS, LANES), jnp.float32)
             for l in range(levels):
                 w = weights_v[j, l]
                 acc_u += w * found[j][0][l]
                 acc_v += w * found[j][1][l]
-            normal = acc_u * cosine + acc_v * sine
-            total = jnp.sum(jnp.sum(normal, axis=0, keepdims=True), axis=1, keepdims=True)
-            speed = total * inverse
+            totals.append(total_of(acc_u * cosine + acc_v * sine))
+        return totals
+
+    def respond(totals, params):
+        results = []
+        for j in range(HOME_MOST):
+            cosine, sine, coef, inverse, square = params[j]
+            speed = totals[j] * inverse
             pull = 0.5 * coef * jnp.abs(speed) * speed
             push = -TIME_STEP * pull
-            results.append((push * cosine, push * sine, pull * speed))
+            gain = push * (cosine * cosine + sine * sine) * square
+            results.append((push * cosine, push * sine, pull * speed, gain))
         return results
 
-    def add_force(get, put, results):
-        for xt in range(x_tiles):
+    def add_force(get, put, results, x_list):
+        for xt in x_list:
             for h in range(halves):
                 scale = []
                 for j in range(HOME_MOST):
@@ -413,19 +422,33 @@
         return get, put
 
     power_row = jnp.zeros((1, LANES), jnp.float32)
-    params = None
+    def add_power(row, results):
+        for j in range(HOME_MOST):
+            row = row + jnp.where(lane1 == j, results[j][2], 0.0)
+        return row
+
+    def send_powers(row):
+        powers[tile] = row * (1.0 / steps)
+        for d in range(1, tiles):
+            power_copy(d).start()
+
+    def wait_gather():
+        for d in range(1, tiles):
+            pltpu.make_async_remote_copy(
+                src_ref=gathered.at[tile],
+                dst_ref=gathered.at[tile_at(tiles - d)],
+                send_sem=gather_send.at[d],
+                recv_sem=gather_recv.at[d],
+                device_id=(layout, tile_at(d)),
+                device_id_type=MESH,
+            ).wait_recv()
+
+    outer = (0, x_tiles - 1)
+    inner = range(1, x_tiles - 1)
+    params, results = None, None
     for step in range(steps):
-        src, dst = step % 2, (step + 1) % 2
+        src = step % 2
         get, put = access(step)
-        results = None
-        if step > 0:
-            results = disk(src, params)
-        if step > 0 and step == steps - 1:
-            for j in range(HOME_MOST):
-                power_row = power_row + jnp.where(lane1 == j, results[j][2], 0.0)
-            powers[tile] = power_row * (1.0 / steps)
-            for d in range(1, tiles):
-                power_copy(d).start()
         lax.fori_loop(
             1, x_tiles - 1, lambda xt, c: (stencil_tile(src, put, xt), c)[1], 0
         )
@@ -437,24 +460,31 @@
             0,
         )
         if step == 0:
-            for d in range(1, tiles):
-                pltpu.make_async_remote_copy(
-                    src_ref=gathered.at[tile],
-                    dst_ref=gathered.at[tile_at(tiles - d)],
-                    send_sem=gather_send.at[d],
-                    recv_sem=gather_recv.at[d],
-                    device_id=(layout, tile_at(d)),
-                    device_id_type=MESH,
-                ).wait_recv()
+            wait_gather()
             params = lay_weights()
-            results = disk(src, params)
-        add_force(get, put, results)
-        if step < steps - 1:
-            for j in range(HOME_MOST):
-                power_row = power_row + jnp.where(lane1 == j, results[j][2], 0.0)
-            pack_edge(step + 1, 0)
-            pack_edge(step + 1, 1)
-            send_edges(step + 1)
+            now = disk(
+                lambda c, l, h, xt: q[src, c, l, h, pl.ds(first + xt * ROWS, ROWS), :],
+                params,
+            )
+            results = respond(now, params)
+            power_row = add_power(power_row, results)
+            if steps == 1:
+                send_powers(power_row)
+        if step == steps - 1:
+            add_force(get, put, results, range(x_tiles))
+            continue
+        ahead = disk(get, params)
+        ahead = [ahead[j] + results[j][3] for j in range(HOME_MOST)]
+        later = respond(ahead, params)
+        power_row = add_power(power_row, later)
+        add_force(get, put, results, outer)
+        pack_edge(step + 1, 0)
+        pack_edge(step + 1, 1)
+        send_edges(step + 1)
+        if step == steps - 2:
+            send_powers(power_row)
+        add_force(get, put, results, inner)
+        results = later
 
     for d in range(1, tiles):
         pltpu.make_async_remote_copy(

time: 19.1 us -> 18.9 us (0.990)
  Pallas kernels: 17.1 us -> 16.8 us
    pallas_call x1, Pallas kernels: 17.1 us -> 16.8 us  [local(): pl.pallas_call(functools.partial(kernel, tiles, layouts, levels, width_x,...]
where the time goes in v4:
time: 18.9 us; the launch traced here: 18.7 us
  Pallas kernels  16.8 us (89%)
  local copies, waits for them, and re-layouts  1.26 us (7%)
  between operations  0.64 us (3%)
    pallas_call x1, Pallas kernels, local(): pl.pallas_call(functools.partial(kernel, tiles, layouts, levels, width_x,...  16.8 us
    unnamed x2, local copies, waits for them, and re-layouts  1.26 us

profile of v4, /device:TPU:0, one launch (start us, length us, event | category | flops | bytes accessed | tf_op | source)
XLA Modules:
  0.0 18.7 jit_solution(7075437060420597284)
XLA Ops:
  0.6 16.8 %shard_map.95 = (f32[1,3,4,32,256]{4,3,2,1,0:T(8,128)S(1)}, f32[1,3]{1,0:T(1,128)S(1)}) custom-call(f32[1,3,4,32,256]{4,3,2,1,0:T(8,128)} %vel_ref.1, f32[1,3,4,256]{3,2,1,0:T(4,128)} %inflow_ref.1, s32[1,40]{1,0:T(1,128)} %site_ref.1, s32[1,40]{1,0:T(1,128)} %block_ref.1, s32[1,40]{1,0:T(1,128)} %slot_ref.1, f32[3,1,512]{2,1,0:T(1,128)} %bitcast.1, ...), custom_call_target="tpu_custom_call" | custom-call | tf_op jit(solution)/shard_map/pallas_call | solution.py:544
  17.5 0.7 %copy.12 = f32[1,3,4,32,256]{4,3,2,1,0:T(8,128)} copy(f32[1,3,4,32,256]{4,3,2,1,0:T(8,128)S(1)} %get-tuple-element.2) | data formatting | bytes 786432
  18.2 0.5 %copy.13 = f32[1,3]{1,0:T(1,128)} copy(f32[1,3]{1,0:T(1,128)S(1)} %get-tuple-element.3) | data formatting | bytes 24

commit v5 on v4

--- a/solution.py
+++ b/solution.py
@@ -477,12 +477,12 @@
         ahead = [ahead[j] + results[j][3] for j in range(HOME_MOST)]
         later = respond(ahead, params)
         power_row = add_power(power_row, later)
+        if step == steps - 2:
+            send_powers(power_row)
         add_force(get, put, results, outer)
         pack_edge(step + 1, 0)
         pack_edge(step + 1, 1)
         send_edges(step + 1)
-        if step == steps - 2:
-            send_powers(power_row)
         add_force(get, put, results, inner)
         results = later
 

time: 18.9 us -> 18.8 us (level)
  no operation moved by 1% of the time
where the time goes in v5:
time: 18.8 us; the launch traced here: 18.6 us
  Pallas kernels  16.7 us (89%)
  local copies, waits for them, and re-layouts  1.26 us (7%)
  between operations  0.64 us (3%)
    pallas_call x1, Pallas kernels, local(): pl.pallas_call(functools.partial(kernel, tiles, layouts, levels, width_x,...  16.7 us
    unnamed x2, local copies, waits for them, and re-layouts  1.26 us

profile of v5, /device:TPU:0, one launch (start us, length us, event | category | flops | bytes accessed | tf_op | source)
XLA Modules:
  0.0 18.6 jit_solution(9060003716457174168)
XLA Ops:
  0.6 16.7 %shard_map.95 = (f32[1,3,4,32,256]{4,3,2,1,0:T(8,128)S(1)}, f32[1,3]{1,0:T(1,128)S(1)}) custom-call(f32[1,3,4,32,256]{4,3,2,1,0:T(8,128)} %vel_ref.1, f32[1,3,4,256]{3,2,1,0:T(4,128)} %inflow_ref.1, s32[1,40]{1,0:T(1,128)} %site_ref.1, s32[1,40]{1,0:T(1,128)} %block_ref.1, s32[1,40]{1,0:T(1,128)} %slot_ref.1, f32[3,1,512]{2,1,0:T(1,128)} %bitcast.1, ...), custom_call_target="tpu_custom_call" | custom-call | tf_op jit(solution)/shard_map/pallas_call | solution.py:544
  17.4 0.7 %copy.12 = f32[1,3,4,32,256]{4,3,2,1,0:T(8,128)} copy(f32[1,3,4,32,256]{4,3,2,1,0:T(8,128)S(1)} %get-tuple-element.2) | data formatting | bytes 786432
  18.1 0.5 %copy.13 = f32[1,3]{1,0:T(1,128)} copy(f32[1,3]{1,0:T(1,128)S(1)} %get-tuple-element.3) | data formatting | bytes 24
